TPU v7x, 32 devices: a whole 2x2x4 slice. The times are simulated.
32 devices in a mesh: groups: 2 (over x), fsdp: 16 (over z, y, core).
Axes of the slice: x: 2, y: 2, z: 4, core: 2. Of those that a mesh axis runs over, the one named last changes fastest.
Arguments:
- hidden_in: bfloat16 [2, 32, 8192], P(None, 'groups', 'fsdp'), parts along dimension 1, may hold values from -6 to 6
- norm_gain: bfloat16 [8192], P('fsdp'), may hold values from 0.099609375 to 1.8984375
- w_query: bfloat16 [8192, 8192], P(None, 'fsdp'), may hold values from -0.0625 to 0.0625
- w_keyval: bfloat16 [8192, 2048], P('fsdp'), may hold values from -0.0625 to 0.0625
- w_out: bfloat16 [8192, 8192], P('fsdp'), may hold values from -0.75 to 0.75
- q_delta: bfloat16 [1536, 128, 128], P(('groups', 'fsdp')), parts along dimension 0, may hold values from -0.125 to 0.125
- q_rows: int32 [1536], P(('groups', 'fsdp')), parts along dimension 0, may hold values from 0 to 63, as said below
- q_cols: int32 [1536], P(('groups', 'fsdp')), parts along dimension 0, may hold values from 0 to 63
- q_count: int32 [32], P(('groups', 'fsdp')), parts along dimension 0, may hold values from 1 to 48, as said below
- o_delta: bfloat16 [1536, 128, 128], P(('groups', 'fsdp')), parts along dimension 0, may hold values from -1 to 1
- o_rows: int32 [1536], P(('groups', 'fsdp')), parts along dimension 0, may hold values from 0 to 63, as said below
- o_cols: int32 [1536], P(('groups', 'fsdp')), parts along dimension 0, may hold values from 0 to 63, as said below
- o_count: int32 [32], P(('groups', 'fsdp')), parts along dimension 0, may hold values from 1 to 48, as said below
- key_cache: bfloat16 [32, 8192, 128], P('groups', 'fsdp'), parts along dimension 0, may hold values from -500 to 500
- value_cache: bfloat16 [32, 8192, 128], P('groups', 'fsdp'), parts along dimension 0, may hold values from -6 to 6
- lengths: int32 [32], P('groups'), parts along dimension 0, may hold values from 1 to 1024, as said below
Outputs:
- attended: bfloat16 [2, 32, 8192], P(None, 'groups', 'fsdp'), parts along dimension 1
There are 2 independent parts, one for each index of `groups`. A program takes and returns all parts, laid end to end along the dimension named above; an argument that names none is the same for every part. Nothing has to cross between parts.
Inputs may be any that keep to these rules, and one draw needn't show every extreme that they name: `q_rows`: slots of owner o name row blocks of that owner's rows o*8192/(128*16) to (o+1)*8192/(128*16)-1; the (row, column) pairs of one owner's slots are distinct. `q_count`: only the first count slots of an owner are live; some owner has 48. `o_rows`: the (row, column) pairs of one owner's slots are distinct. `o_cols`: slots of owner o name column blocks of that owner's columns o*8192/(128*16) to (o+1)*8192/(128*16)-1. `o_count`: only the first count slots of an owner are live; some owner has 48. `lengths`: some sequence has 1024.
All inputs are finite; a program needn't handle non-finite values.
Results may differ from a plain program's by a relative error of at most 0.012.
The roundings to bfloat16 on the way count: a program that leaves them out, or rounds other values in their place, can miss the bound.
Values may be sent and summed in bfloat16 or wider, within the bound.
A program may use at most 128 MiB of HBM per device.

v0:
```python
import jax
import jax.numpy as jnp
from jax import lax
from jax.sharding import PartitionSpec as P

D = 8192
HEADS = 64
KVH = 8
HD = 128
BLOCK = 128


theta_base = 1000000.0
eps = 1e-06
masked = -1e30


def from_partner(array, axis, bit):
    return lax.ppermute(array, axis, [(i, i ^ 1 << bit) for i in range(lax.axis_size(axis))])


def for_sending(array):
    return jax.tree.map(lambda a: a.astype(jnp.bfloat16) if a.dtype == jnp.float32 else a, array)


def rotate(vec, position):
    half = vec.shape[-1] // 2
    freq = theta_base ** (-(jnp.arange(half, dtype=jnp.float32) * 2.0) / vec.shape[-1])
    angle = position[..., None] * freq
    cosine = jnp.cos(angle)
    sine = jnp.sin(angle)
    first = vec[..., :half]
    second = vec[..., half:]
    return jnp.concatenate(
        [first * cosine - second * sine, second * cosine + first * sine], axis=-1
    )


def spread_blocks(values, spots, live_count, total):
    slots = values.shape[0]
    alive = jnp.arange(slots, dtype=jnp.int32) < live_count
    table = (
        (spots[None, :] == jnp.arange(total, dtype=jnp.int32)[:, None]) & alive[None, :]
    ).astype(jnp.bfloat16)
    flat = values.reshape(slots, -1)
    return jnp.dot(table, flat, preferred_element_type=jnp.float32).astype(jnp.bfloat16)


def combine(first, second):
    top = jnp.maximum(first[0], second[0])
    left = jnp.exp(first[0] - top)
    right = jnp.exp(second[0] - top)
    return (
        top,
        first[1] * left + second[1] * right,
        first[2] * left[..., None] + second[2] * right[..., None],
    )


def local(
    hidden_in,
    norm_gain,
    w_query,
    w_keyval,
    w_out,
    q_delta,
    q_rows,
    q_cols,
    q_count,
    o_delta,
    o_rows,
    o_cols,
    o_count,
    key_cache,
    value_cache,
    lengths,
):
    count = lax.axis_size("fsdp")
    me = lax.axis_index("fsdp")
    row_blocks = D // BLOCK // count
    col_blocks = HEADS * HD // BLOCK // count
    inner = row_blocks * col_blocks
    query_spots = (
        q_cols // col_blocks * row_blocks + q_rows - me * row_blocks
    ) * col_blocks + q_cols % col_blocks
    out_spots = o_rows * row_blocks + o_cols - me * row_blocks
    query_dense = spread_blocks(q_delta, query_spots, q_count[0], count * inner)
    out_dense = spread_blocks(o_delta, out_spots, o_count[0], count * inner)
    outgoing = jnp.concatenate(
        [
            query_dense.reshape(count, inner, BLOCK, BLOCK),
            out_dense.reshape(count, inner, BLOCK, BLOCK),
        ],
        axis=1,
    )
    incoming = lax.all_to_all(outgoing, "fsdp", split_axis=0, concat_axis=0, tiled=True)
    query_part = (
        incoming[:, :inner]
        .reshape(count, row_blocks, col_blocks, BLOCK, BLOCK)
        .transpose(0, 1, 3, 2, 4)
        .reshape(D, col_blocks * BLOCK)
    )
    out_part = (
        incoming[:, inner:]
        .reshape(count, col_blocks, row_blocks, BLOCK, BLOCK)
        .transpose(1, 3, 0, 2, 4)
        .reshape(col_blocks * BLOCK, D)
    )
    merged_q = (w_query.astype(jnp.float32) + query_part.astype(jnp.float32)).astype(jnp.bfloat16)
    merged_o = (w_out.astype(jnp.float32) + out_part.astype(jnp.float32)).astype(jnp.bfloat16)
    whole_x, whole_gain = (
        lax.all_gather(hidden_in, "fsdp", axis=2, tiled=True),
        lax.all_gather(norm_gain, "fsdp", axis=0, tiled=True),
    )
    steps = whole_x.shape[0]
    seqs = whole_x.shape[1]
    xf = whole_x.astype(jnp.float32)
    power = jnp.mean(xf * xf, axis=-1, keepdims=True)
    normed = (xf * lax.rsqrt(power + eps) * whole_gain.astype(jnp.float32)).astype(jnp.bfloat16)
    flat = normed.reshape(steps * seqs, D)
    position = (lengths[None, :] + jnp.arange(steps, dtype=jnp.int32)[:, None]).astype(jnp.float32)
    per_device = HEADS // count
    query = jnp.dot(flat, merged_q, preferred_element_type=jnp.float32).reshape(
        steps, seqs, per_device, HD
    )
    query = (
        rotate(query, position[:, :, None])
        .astype(jnp.bfloat16)
        .reshape(steps, seqs, per_device * HD)
    )
    width = D // count
    local_rows = lax.dynamic_slice_in_dim(flat, me * width, width, 1)
    keyval = lax.psum(jnp.dot(local_rows, w_keyval, preferred_element_type=jnp.float32), "fsdp")
    split = count // KVH
    head_group = me // split
    member = me % split
    group = HEADS // KVH
    key_part = lax.dynamic_slice_in_dim(keyval, head_group * HD, HD, 1).reshape(steps, seqs, HD)
    value_part = lax.dynamic_slice_in_dim(keyval, KVH * HD + head_group * HD, HD, 1).reshape(
        steps, seqs, HD
    )
    new_keys = rotate(key_part, position).astype(jnp.bfloat16)
    new_values = value_part.astype(jnp.bfloat16)
    group_query = query
    for bit in range(split.bit_length() - 1):
        partner = from_partner(group_query, "fsdp", bit)
        upper = me >> bit & 1 == 1
        group_query = jnp.where(
            upper,
            jnp.concatenate([partner, group_query], axis=2),
            jnp.concatenate([group_query, partner], axis=2),
        )
    group_query = group_query.reshape(steps, seqs, group, HD)
    scale = HD ** (-0.5)
    span = key_cache.shape[1]
    spots = member * span + jnp.arange(span, dtype=jnp.int32)
    valid_cache = (spots[None, :] < lengths[:, None])[None, :, None, :]
    stepping = jnp.arange(steps, dtype=jnp.int32)
    valid_new = ((stepping[None, :] <= stepping[:, None]) & (member == 0))[:, None, None, :]
    cache_scores = (
        jnp.einsum("tshd,scd->tshc", group_query, key_cache, preferred_element_type=jnp.float32)
        * scale
    )
    new_scores = (
        jnp.einsum("tshd,usd->tshu", group_query, new_keys, preferred_element_type=jnp.float32)
        * scale
    )
    cache_scores = jnp.where(valid_cache, cache_scores, masked)
    new_scores = jnp.where(valid_new, new_scores, masked)
    top = jnp.maximum(jnp.max(cache_scores, -1), jnp.max(new_scores, -1))
    cache_weights = jnp.where(valid_cache, jnp.exp(cache_scores - top[..., None]), 0.0)
    new_weights = jnp.where(valid_new, jnp.exp(new_scores - top[..., None]), 0.0)
    totals = jnp.sum(cache_weights, -1) + jnp.sum(new_weights, -1)
    mixed = jnp.einsum(
        "tshc,scd->tshd",
        cache_weights.astype(jnp.bfloat16),
        value_cache,
        preferred_element_type=jnp.float32,
    )
    mixed = mixed + jnp.einsum(
        "tshu,usd->tshd",
        new_weights.astype(jnp.bfloat16),
        new_values,
        preferred_element_type=jnp.float32,
    )
    state = (top, totals, mixed)
    for bit in range(split.bit_length() - 1):
        partner = from_partner(
            (for_sending(state[0]), for_sending(state[1]), for_sending(state[2])), "fsdp", bit
        )
        state = combine(state, partner)
    totals = state[1]
    mixed = state[2]
    heads_out = (mixed / totals[..., None]).astype(jnp.bfloat16)
    mine = lax.dynamic_slice_in_dim(heads_out, member * per_device, per_device, 2).reshape(
        steps * seqs, per_device * HD
    )
    partial_out = jnp.dot(mine, merged_o, preferred_element_type=jnp.float32).reshape(
        steps, seqs, D
    )
    return lax.psum_scatter(partial_out, "fsdp", scatter_dimension=2, tiled=True).astype(
        jnp.bfloat16
    )


def solution(mesh):
    in_specs = (
        P(None, "groups", "fsdp"),
        P("fsdp"),
        P(None, "fsdp"),
        P("fsdp", None),
        P("fsdp", None),
        P(("groups", "fsdp"), None, None),
        P(("groups", "fsdp")),
        P(("groups", "fsdp")),
        P(("groups", "fsdp")),
        P(("groups", "fsdp"), None, None),
        P(("groups", "fsdp")),
        P(("groups", "fsdp")),
        P(("groups", "fsdp")),
        P("groups", "fsdp", None),
        P("groups", "fsdp", None),
        P("groups"),
    )
    out_specs = P(None, "groups", "fsdp")
    return jax.shard_map(local, mesh=mesh, in_specs=in_specs, out_specs=out_specs, check_vma=False)
```

profile of v0, /device:TPU:29, one launch (start us, length us, event | category | flops | bytes accessed | tf_op | source)
XLA Modules:
  0.0 709.4 jit_solution(17171559458512877663)
XLA Ops:
  6.5 0.0 copy-start
  7.4 0.7 fusion.66
  8.1 7.0 fusion.5
  15.1 0.0 copy-start.2
  15.1 9.3 %copy.78 = bf16[32,8,128,128]{3,2,1,0:T(8,128)(2,1)} copy(bf16[32,8,128,128]{3,1,2,0:T(8,128)(2,1)} %fusion.5) | data formatting | bytes 16777216
  25.0 0.0 copy-done.2
  25.0 5.6 fusion.6
  30.6 9.2 %copy.80 = bf16[32,8,128,128]{3,2,1,0:T(8,128)(2,1)} copy(bf16[32,8,128,128]{3,1,2,0:T(8,128)(2,1)} %fusion.6) | data formatting | bytes 16777216
  39.8 13.7 %pad_maximum_fusion = bf16[16,32,128,128]{3,2,1,0:T(8,128)(2,1)} fusion(bf16[16,16,128,128]{3,2,1,0:T(8,128)(2,1)} %bitcast.121, bf16[16,16,128,128]{3,2,1,0:T(8,128)(2,1)} %bitcast.120), kind=kLoop, calls=%fused_computation.4 | loop fusion | flops 8388608 | bytes 33554432 | tf_op jit(solution)/shard_map/concatenate | solution.py:89
  53.5 0.0 copy-start.3
  53.5 0.0 copy-start.5
  53.5 6.5 all-to-all-start
  60.0 0.0 all-reduce.2.cloned.1.call-start
  60.0 0.0 copy-done.4
  60.1 370.6 %all-gather = bf16[16,1,512]{2,1,0:T(2,128)(2,1)S(1)} all-gather(bf16[1,1,512]{2,1,0:T(2,128)(2,1)S(1)} %reshape.187), channel_id=1, replica_groups=mesh['groups'=2,'fsdp'=16] {'fsdp'}, dimensions={0}, use_global_device_ids=true | all-gather | bytes 17408 | tf_op jit(solution)/shard_map/all_gather | solution.py:113
  430.7 0.0 copy-done.3
  430.7 17.7 %all_gather.6 = bf16[2,16,8192]{2,1,0:T(8,128)(2,1)S(1)} all-gather(bf16[2,16,512]{2,1,0:T(8,128)(2,1)S(1)} %copy-done.3), channel_id=1, replica_groups=mesh['groups'=2,'fsdp'=16] {'fsdp'}, dimensions={2}, use_global_device_ids=true | all-gather | bytes 557056 | tf_op jit(solution)/shard_map/all_gather | solution.py:112
  448.4 0.2 fusion.32
  448.6 0.2 fusion.34
  448.8 2.8 fusion.57
  451.6 0.0 all-reduce.2.cloned.1.call-update
  451.6 0.2 reduce-scatter.2.cloned.1.call-start
  451.9 0.0 copy-done.5
  451.9 0.1 broadcast_compare_fusion
  452.0 89.2 %all-reduce.2.cloned.1.call-done = f32[32,2048]{1,0:T(8,128)} async-done(((f32[32,2048]{1,0:T(8,128)}), f32[32,2048]{1,0:T(8,128)}) %all-reduce.2.cloned.1.call-update) | async-done | bytes 262160 | tf_op jit(solution)/shard_map/psum | solution.py:133
  541.2 0.7 constant_dynamic-slice_fusion.3
  542.0 0.1 subtract_convert_fusion
  542.1 0.1 maximum_bitcast_fusion
  542.2 0.7 dynamic-slice_convert_fusion
  542.9 0.0 all-to-all-done
  542.9 9.6 %fusion.72 = (bf16[16,16,128,128]{3,2,1,0:T(8,128)(2,1)S(1)}, bf16[16,16,128,128]{3,2,1,0:T(8,128)(2,1)}) fusion(bf16[16,32,128,128]{3,2,1,0:T(8,128)(2,1)} %all-to-all-done), kind=kLoop, calls=%fused_computation.105 | loop fusion | bytes 33554432 | tf_op jit(solution)/shard_map/slice | solution.py:98
  552.5 6.8 copy.53
  559.3 9.3 %fusion.2 = bf16[512,8192]{0,1:T(8,128)(2,1)} fusion(f32[1024,8,4,128]{3,2,1,0:T(4,128)S(1)} %bitcast.115, bf16[8192,512]{1,0:T(8,128)(2,1)} %param.18), kind=kLoop, calls=%fused_computation.8 | loop fusion | flops 12582912 | bytes 33554432 | tf_op jit(solution)/shard_map/dot_general | solution.py:123
  568.6 12.0 %copy.69 = bf16[512,8192]{1,0:T(8,128)(2,1)} copy(bf16[512,8192]{0,1:T(8,128)(2,1)} %fusion.2) | data formatting | bytes 16777216 | tf_op jit(solution)/shard_map/dot_general | solution.py:123
  580.6 6.1 fusion.35
  586.7 0.1 multiply_subtract_fusion
  586.9 0.1 copy_bitcast_fusion.1
  586.9 1.4 collective-permute-start
  588.4 0.1 maximum_convert_fusion
  588.5 0.0 copy-done.1
  588.5 20.9 %copy.112 = f32[16,4,4,128,128]{4,2,0,3,1:T(4,128)} copy(bf16[16,4,4,128,128]{4,3,2,1,0:T(8,128)(2,1)S(1)} %bitcast.117) | data formatting | bytes 25165824 | tf_op jit(solution)/shard_map/convert_element_type | solution.py:110
  609.4 20.3 %reshape.184 = f32[512,8192]{1,0:T(8,128)} reshape(f32[4,128,16,4,128]{4,3,2,1,0:T(4,128)} %bitcast.116) | data formatting | bytes 33554432 | tf_op jit(solution)/shard_map/convert_element_type | solution.py:110
  629.7 0.0 collective-permute-done
  629.7 0.0 copy-done
  629.7 0.8 fusion.73
  630.5 0.4 fusion.74
  630.9 0.1 fusion.65
  631.1 0.3 fusion.37
  631.3 0.1 collective-permute-start.3
  631.4 0.5 collective-permute-start.1
  631.9 0.3 convolution_bitcast_fusion
  632.2 2.1 fusion.75
  634.3 0.1 collective-permute-start.2
  634.4 0.0 collective-permute-done.3
  634.4 0.0 collective-permute-done.1
  634.4 0.1 constant_dynamic-slice_fusion
  634.5 0.1 constant_dynamic-slice_fusion.1
  634.6 0.1 constant_dynamic-slice_fusion.2
  634.7 0.9 collective-permute-done.2
  635.6 0.2 fusion.51
  635.8 10.9 %fusion.3 = f32[2,16,8192]{2,1,0:T(8,128)} fusion(f32[512,8192]{1,0:T(8,128)} %reshape.184, bf16[512,8192]{1,0:T(8,128)(2,1)} %param.20, bf16[2,16,512]{2,0,1:T(2,128)(2,1)S(1)} %reshape.197), kind=kOutput, calls=%fused_computation.9 | convolution fusion | flops 281018368 | bytes 26247168 | tf_op jit(solution)/shard_map/dot_general | solution.py:198
  646.7 0.0 reduce-scatter.2.cloned.1.call-update
  646.7 54.4 %reduce-scatter.2.cloned.1.call-done = f32[2,16,512]{2,1,0:T(8,128)} async-done(((f32[2,16,8192]{2,1,0:T(8,128)}), f32[2,16,512]{2,1,0:T(8,128)}) %reduce-scatter.2.cloned.1.call-update) | async-done | bytes 65552 | tf_op jit(solution)/shard_map/reduce_scatter | solution.py:201
  701.1 1.5 convert_element_type.141
  (17 shorter events, 0.2 us)
Async XLA Ops:
  6.5 623.2 %copy-start = (bf16[16,512,128]{2,1,0:T(8,128)(2,1)S(1)}, bf16[16,512,128]{2,1,0:T(8,128)(2,1)}, u32[]{:S(2)}) copy-start(bf16[16,512,128]{2,1,0:T(8,128)(2,1)} %param.29) | copy-start | bytes 6291460
  15.1 10.0 %copy-start.2 = (bf16[48,128,128]{2,1,0:T(8,128)(2,1)S(1)}, bf16[48,128,128]{2,1,0:T(8,128)(2,1)}, u32[]{:S(2)}) copy-start(bf16[48,128,128]{2,1,0:T(8,128)(2,1)} %param.25) | copy-start | bytes 4718596
  53.5 6.5 copy-start.4
  53.5 377.2 %copy-start.3 = (bf16[2,16,512]{2,1,0:T(8,128)(2,1)S(1)}, bf16[2,16,512]{2,1,0:T(8,128)(2,1)}, u32[]{:S(2)}) copy-start(bf16[2,16,512]{2,1,0:T(8,128)(2,1)} %param.16) | copy-start | bytes 98308
  53.5 398.4 %copy-start.5 = (s32[16]{0:T(128)S(1)}, s32[16]{0:T(128)}, u32[]{:S(2)}) copy-start(s32[16]{0:T(128)} %param.31) | copy-start | bytes 196
  53.5 489.4 %all-to-all-start = ((bf16[16,32,128,128]{3,2,1,0:T(8,128)(2,1)}), bf16[16,32,128,128]{3,2,1,0:T(8,128)(2,1)}, u32[]{:S(2)}, u32[]{:S(2)}) async-start(bf16[16,32,128,128]{3,2,1,0:T(8,128)(2,1)} %pad_maximum_fusion), calls=%async_computation | async-start | bytes 33554432 | tf_op jit(solution)/shard_map/all_to_all | solution.py:96
  60.0 481.2 %all-reduce.2.cloned.1.call-start = ((), (), s32[]{:S(2)}) async-start(), calls=%async_computation.2 | async-start | bytes 524288 | tf_op jit(solution)/shard_map/psum | solution.py:133
  451.6 249.5 %reduce-scatter.2.cloned.1.call-start = ((), (), s32[]{:S(2)}) async-start(), calls=%async_computation.3 | async-start | bytes 1114112 | tf_op jit(solution)/shard_map/reduce_scatter | solution.py:201
  580.6 7.9 %copy-start.1 = (bf16[16,16,128,128]{3,2,1,0:T(8,128)(2,1)S(1)}, bf16[16,16,128,128]{3,2,1,0:T(8,128)(2,1)}, u32[]{:S(2)}) copy-start(bf16[16,16,128,128]{3,2,1,0:T(8,128)(2,1)} %get-tuple-element.11) | copy-start | bytes 25165828
  586.9 42.7 %collective-permute-start = (bf16[2,16,512]{2,1,0:T(8,128)(2,1)S(1)}, bf16[2,16,512]{2,1,0:T(8,128)(2,1)S(1)}, u32[]{:S(2)}, u32[]{:S(2)}) collective-permute-start(bf16[2,16,512]{2,1,0:T(8,128)(2,1)S(1)} %copy_bitcast_fusion.1), channel_id=1, source_target_pairs={{0,1},{1,0},{2,3},{3,2},{4,5},{5,4},{6,7},{7,6},{8,9},{9,8},{10,11... | collective-permute-start | bytes 98312 | tf_op jit(solution)/shard_map/ppermute | solution.py:19
  631.3 3.1 collective-permute-start.3
  631.4 3.0 collective-permute-start.1
  634.3 1.3 collective-permute-start.2
Sparse Core Ops, SparseCore 0:
  451.7 89.4 all-reduce.1
  646.9 54.2 reduce-scatter.1
where the time goes:
time: 716 us; the launch traced here: 709 us
  blocking collectives  388 us (54%)
  waiting for transfers between devices  145 us (20%)
  local copies, waits for them, and re-layouts  89.9 us (13%)
  matrix products  35.9 us (5%)
  other arithmetic  26.8 us (4%)
  between operations  15.1 us (2%)
  starting transfers between devices  8.88 us (1%)
    all_gather x1, blocking collectives, local(): lax.all_gather(norm_gain, 'fsdp', axis=0, tiled=True)  371 us
    psum x1, waiting for transfers between devices, local(): lax.psum(jnp.dot(local_rows, w_keyval, preferred_element_type=jnp.float32...  89.2 us
    reduce_scatter x1, waiting for transfers between devices, local(): lax.psum_scatter(partial_out, 'fsdp', scatter_dimension=2, tiled=True)  54.4 us
    convert_element_type x2, local copies, waits for them, and re-layouts, local(): out_part.astype(jnp.float32)  41.2 us
    unnamed x15, local copies, waits for them, and re-layouts  18.5 us
    all_gather x1, blocking collectives, local(): lax.all_gather(hidden_in, 'fsdp', axis=2, tiled=True)  17.7 us
  transfers between devices with their start and end apart: 7, of which 3 were waited for; matrix products, arithmetic and copies ran while one was open for 7% of the time, Pallas kernels for 0%

commit v1 on v0

v1 whole, which is shorter than its diff:
```python
import functools

import jax
import jax.numpy as jnp
from jax import lax
from jax.experimental import pallas as pl
from jax.experimental.pallas import tpu as pltpu
from jax.sharding import PartitionSpec as P

HD = 128
BLOCK = 128
theta_base = 1000000.0
eps = 1e-06
masked = -1e30
MESH = pl.DeviceIdType.MESH
F32 = jnp.float32
BF16 = jnp.bfloat16
VM = pl.BlockSpec(memory_space=pltpu.VMEM)
SM = pl.BlockSpec(memory_space=pltpu.SMEM)
ANY = pl.BlockSpec(memory_space=pl.ANY)


def rcopy(src, dst, send, recv, device):
    return pltpu.make_async_remote_copy(
        src_ref=src, dst_ref=dst, send_sem=send, recv_sem=recv,
        device_id={"fsdp": device}, device_id_type=MESH,
    )


def greet(devices):
    barrier = pltpu.get_barrier_semaphore()
    for device in devices:
        pl.semaphore_signal(barrier, inc=1, device_id={"fsdp": device}, device_id_type=MESH)
    pl.semaphore_wait(barrier, len(devices))


def spread(n, me, buf, start, size, sems):
    chips = n // 2
    chip, core = me // 2, me % 2
    partner = me + 1 - 2 * core
    ss, sr, fs, fr = sems
    view = lambda dev: buf.at[pl.ds(dev * size, size)]
    out = []
    for d in range(1, chips):
        dst = 2 * ((chip + d) % chips) + core
        c = rcopy(view(me), view(me), ss.at[d], sr.at[d], dst)
        c.start()
        out.append(c)
    c = rcopy(view(me), view(me), fs.at[0], fr.at[0], partner)
    c.start()
    forwards = [c]
    return out, forwards


def pass_on(n, me, buf, size, sems, out, forwards):
    chips = n // 2
    chip, core = me // 2, me % 2
    partner = me + 1 - 2 * core
    ss, sr, fs, fr = sems
    for d in range(1, chips):
        out[d - 1].wait_recv()
        src = 2 * ((chip + chips - d) % chips) + core
        v = buf.at[pl.ds(src * size, size)]
        c = rcopy(v, v, fs.at[d], fr.at[d], partner)
        c.start()
        forwards.append(c)
    for c in forwards:
        c.wait_recv()
    for c in out + forwards:
        c.wait_send()


def rope(v, cosine, sine):
    return v * cosine + pltpu.roll(v, HD // 2, 1) * sine


def pack_kernel(
    cap, row_blocks, per, rows_ref, cols_ref, count_ref, delta_ref, pack_ref, place_ref, over_ref, seen_ref
):
    me = lax.axis_index("fsdp")
    n = place_ref.shape[0]
    pack_ref[...] = jnp.zeros_like(pack_ref)
    place_ref[...] = jnp.zeros_like(place_ref)
    for j in range(n):
        seen_ref[j] = 0
    count = count_ref[0]

    @pl.loop(0, delta_ref.shape[0])
    def _(k):
        c = cols_ref[k]
        j = lax.div(c, per)
        seen = seen_ref[j]
        live = k < count
        fits = jnp.logical_and(live, seen < cap)
        over_ref[k] = jnp.where(jnp.logical_and(live, seen >= cap), 1, 0)

        @pl.when(fits)
        def _():
            pack_ref[j * cap + seen] = delta_ref[k]
            spot = (rows_ref[k] - me * row_blocks) * per + lax.rem(c, per)
            place_ref[j, pl.ds(seen, 1), :] = jnp.full((1, 128), spot, jnp.int32).astype(F32)
            seen_ref[j] = seen + 1


def gather_kernel(
    n, cap, x_ref, gain_ref, wq_hbm, wkv_hbm, pack_ref, place_ref,
    all_ref, q_ref, kv_ref, blocks_ref, places_ref,
    buf, wq, wkv, blocks, places, ss, sr, fs, fr, ws, ds, dr, ms, mr,
):
    me = lax.axis_index("fsdp")
    rows, feats = x_ref.shape
    chips = n // 2
    chip, core = me // 2, me % 2
    load_q = pltpu.make_async_copy(wq_hbm, wq, ws.at[0])
    load_kv = pltpu.make_async_copy(wkv_hbm, wkv, ws.at[1])
    load_q.start()
    load_kv.start()
    buf[me, 0:rows, :] = x_ref[...]
    buf[me, rows : rows + 16, :] = jnp.broadcast_to(
        gain_ref[...].astype(F32), (16, feats)
    ).astype(BF16)
    greet([(me + d) % n for d in range(1, n)])
    sems = (ss, sr, fs, fr)
    out, forwards = spread(n, me, buf, None, 1, sems)
    sent = []
    for d in range(1, n):
        dst = (me + d) % n
        c = rcopy(place_ref.at[dst], places.at[me], ms.at[d], mr.at[d], dst)
        c.start()
        sent.append(c)
        c = rcopy(
            pack_ref.at[pl.ds(dst * cap, cap)], blocks.at[pl.ds(me * cap, cap)], ds.at[d], dr.at[d], dst
        )
        c.start()
        sent.append(c)
    places[me] = place_ref[me]
    for i in range(cap):
        blocks[me * cap + i] = pack_ref[me * cap + i]
    pass_on(n, me, buf, 1, sems, out, forwards)

    def squares(j, total):
        v = buf[j, 0:rows, :].astype(F32)
        return total + jnp.sum(v * v, axis=-1, keepdims=True)

    power = lax.fori_loop(0, n, squares, jnp.zeros((rows, 1), F32)) / (n * feats)
    factor = lax.rsqrt(power + eps)

    def normed(j):
        v = buf[j, 0:rows, :].astype(F32)
        g = buf[j, rows : rows + 16, :].astype(F32)[0:1]
        return (v * factor * g).astype(BF16)

    own = normed(me)
    load_kv.wait()
    kv_ref[...] = jnp.dot(own, wkv[...], preferred_element_type=F32)
    load_q.wait()
    q_ref[...] = jnp.zeros_like(q_ref)

    @pl.loop(0, n)
    def _(j):
        w = wq[pl.ds(pl.multiple_of(j * feats, feats), feats), :]
        v = normed(j)
        for r in range(feats // BLOCK):
            all_ref[j * (feats // BLOCK) + r] = v[:, r * BLOCK : (r + 1) * BLOCK]
        q_ref[...] += jnp.dot(v, w, preferred_element_type=F32)

    for c in sent:
        c.wait()
    blocks_ref[...] = blocks[...]
    places_ref[...] = places[...]


def query_delta_kernel(
    n, split, unroll, cap, rows_ref, cols_ref, over_ref, spot_ref, all_ref, kv_ref, delta_ref,
    q_ref, w_ref, got_ref, msg_ref, query_ref
):
    me = lax.axis_index("fsdp")
    blocks = all_ref.shape[0] // n
    slots = delta_ref.shape[0]
    width = msg_ref.shape[2] - HD
    per = width // BLOCK
    half = kv_ref.shape[1] // 2
    for j in range(n):
        at = (j % 2) * half + (j // split) * HD
        msg_ref[j, :, 0:width] = jnp.zeros((msg_ref.shape[1], width), F32)
        msg_ref[j, :, width : width + HD] = kv_ref[:, at : at + HD]
    query_ref[...] = q_ref[...]
    group = next(u for u in (8, 4, 2, 1) if (n * cap) % u == 0)

    @pl.loop(0, n * cap // group)
    def _(step):
        done = []
        for u in range(group):
            e = step * group + u
            spot = spot_ref[e]
            r = lax.div(e, cap) * blocks + lax.div(spot, per)
            at = pl.ds(pl.multiple_of(lax.rem(spot, per) * BLOCK, BLOCK), BLOCK)
            base = w_ref[pl.ds(pl.multiple_of(r * BLOCK, BLOCK), BLOCK), at]
            merged = (base.astype(F32) + got_ref[e].astype(F32)).astype(BF16)
            lhs = all_ref[r]
            done.append(
                (
                    at,
                    jnp.dot(lhs, merged, preferred_element_type=F32)
                    - jnp.dot(lhs, base, preferred_element_type=F32),
                )
            )
        for at, term in done:
            query_ref[:, at] = query_ref[:, at] + term

    @pl.loop(0, slots // unroll)
    def _(step):
        done = []
        for u in range(unroll):
            k = step * unroll + u
            r = jnp.clip(rows_ref[k] - me * blocks, 0, blocks - 1)
            lhs = all_ref[me * blocks + r]
            lhs = jnp.where(over_ref[k] > 0, lhs, jnp.zeros_like(lhs))
            done.append(jnp.dot(lhs, delta_ref[k], preferred_element_type=F32))
        for u in range(unroll):
            c = cols_ref[step * unroll + u]
            at = pl.ds(pl.multiple_of(lax.rem(c, per) * BLOCK, BLOCK), BLOCK)
            j = lax.div(c, per)
            msg_ref[j, :, at] = msg_ref[j, :, at] + done[u]


def out_delta_kernel(unroll, rows_ref, cols_ref, count_ref, heads_ref, base_ref, delta_ref, out_ref, acc):
    me = lax.axis_index("fsdp")
    slots = delta_ref.shape[0]
    blocks = base_ref.shape[1] // BLOCK
    acc[...] = base_ref[...]
    count = count_ref[0]

    @pl.loop(0, slots // unroll)
    def _(step):
        done = []
        for u in range(unroll):
            k = step * unroll + u
            lhs = heads_ref[rows_ref[k]]
            lhs = jnp.where(k < count, lhs, jnp.zeros_like(lhs))
            done.append(jnp.dot(lhs, delta_ref[k], preferred_element_type=F32))
        for u in range(unroll):
            c = jnp.clip(cols_ref[step * unroll + u] - me * blocks, 0, blocks - 1)
            at = pl.ds(pl.multiple_of(c * BLOCK, BLOCK), BLOCK)
            acc[:, at] = acc[:, at] + done[u]

    out_ref[...] = acc[...].astype(BF16)


def main_kernel(
    n, split, steps, msg, q_ref, cos_ref, sin_ref, len_ref, keys_hbm, values_hbm, wout_hbm,
    heads_out, base_out,
    keys, values, wout, got_a, held_b, got_b, shared, queries, parts, got_parts, mine,
    out_a, out_got_a, out_b, out_got_b, heads,
    ws, as_, ar, bs, br, es, er, ps, pr, oas, oar, obs, obr, ss, sr, fs, fr,
):
    me = lax.axis_index("fsdp")
    chips = n // 2
    chip, core = me // 2, me % 2
    partner = me + 1 - 2 * core
    member = me % split
    first = me - member
    rows, width = q_ref.shape
    per = width // HD
    group = per * split
    seqs = rows // steps
    span = keys.shape[1]
    feats = base_out.shape[1]

    loads = [
        pltpu.make_async_copy(keys_hbm, keys, ws.at[0]),
        pltpu.make_async_copy(values_hbm, values, ws.at[1]),
        pltpu.make_async_copy(wout_hbm, wout, ws.at[2]),
    ]
    for c in loads:
        c.start()
    chip_at = lambda d: (chip + d) % chips
    same = lambda d: 2 * chip_at(d) + core
    mate = lambda e: first + (member + e) % split
    greet([same(d) for d in range(1, chips)] + [mate(e) for e in range(1, split, 2)])

    order = list(range(1, chips)) + [0]
    a = {}
    for d in order:
        a[d] = rcopy(msg.at[2 * chip_at(d) + 1 - core], got_a.at[d], as_.at[d], ar.at[d], partner)
        a[d].start()
    b = {}
    for d in order:
        a[d].wait_recv()
        held_b[d] = msg[2 * chip_at(d) + core] + got_a[d]
        if d:
            b[d] = rcopy(held_b.at[d], got_b.at[d], bs.at[d], br.at[d], same(d))
            b[d].start()
    total = held_b[0]
    for d in range(1, chips):
        b[d].wait_recv()
        total = total + got_b[d]
    cosine, sine = cos_ref[...], sin_ref[...]
    for h in range(per):
        at = slice(h * HD, (h + 1) * HD)
        v = q_ref[:, at] + total[:, at]
        shared[member, :, at] = rope(v, cosine, sine).astype(BF16)
    kv = total[:, width:]
    plain = jnp.broadcast_to(core, kv.shape) == 1
    shared[member, :, width:] = jnp.where(plain, kv, rope(kv, cosine, sine)).astype(BF16)
    ex = []
    for e in range(1, split):
        c = rcopy(shared.at[member], shared.at[member], es.at[e], er.at[e], mate(e))
        c.start()
        ex.append(c)
    for c in ex:
        c.wait_recv()

    for h in range(group):
        at = slice((h % per) * HD, (h % per + 1) * HD)
        queries[h * rows : (h + 1) * rows, :] = shared[h // per, :, at].astype(F32)
    loads[0].wait()
    loads[1].wait()
    scale = HD ** (-0.5)
    spots = member * span + lax.broadcasted_iota(jnp.int32, (group * steps, span), 1)
    for s in range(seqs):
        at = pl.ds(s, group * steps, stride=seqs)
        q = queries[at, :].astype(BF16)
        score = (
            lax.dot_general(q, keys[s], (((1,), (1,)), ((), ())), preferred_element_type=F32)
            * scale
        )
        valid = spots < len_ref[s]
        score = jnp.where(valid, score, masked)
        top = jnp.max(score, axis=-1, keepdims=True)
        weight = jnp.where(valid, jnp.exp(score - top), 0.0)
        shape = (group * steps, HD)
        parts[0, at, :] = jnp.dot(weight.astype(BF16), values[s], preferred_element_type=F32)
        parts[1, at, :] = jnp.broadcast_to(top, shape)
        parts[2, at, :] = jnp.broadcast_to(jnp.sum(weight, axis=-1, keepdims=True), shape)
    chunk = per * rows
    px = []
    for e in range(1, split):
        dst = (member + e) % split
        c = rcopy(
            parts.at[:, pl.ds(dst * chunk, chunk), :], got_parts.at[e], ps.at[e], pr.at[e], mate(e)
        )
        c.start()
        px.append(c)

    new_keys = shared[0, :, width:].astype(F32)
    new_values = shared[1, :, width:].astype(F32)
    step_of = lax.broadcasted_iota(jnp.int32, (rows, 1), 0) // seqs
    fresh = []
    for h in range(per):
        q = shared[member, :, h * HD : (h + 1) * HD].astype(F32)
        scores = []
        for u in range(steps):
            k = jnp.concatenate([new_keys[u * seqs : (u + 1) * seqs]] * steps, axis=0)
            sc = jnp.sum(q * k, axis=-1, keepdims=True) * scale
            scores.append(jnp.where(step_of >= u, sc, masked))
        top = functools.reduce(jnp.maximum, scores)
        tot = jnp.zeros_like(top)
        mix = jnp.zeros((rows, HD), F32)
        for u in range(steps):
            v = jnp.concatenate([new_values[u * seqs : (u + 1) * seqs]] * steps, axis=0)
            w = jnp.where(step_of >= u, jnp.exp(scores[u] - top), 0.0)
            tot = tot + w
            mix = mix + w.astype(BF16).astype(F32) * v
        fresh.append((mix, top, tot))
    for c in px:
        c.wait_recv()
    for h in range(per):
        own = pl.ds(pl.multiple_of(member * chunk + h * rows, rows), rows)
        states = [fresh[h], (parts[0, own, :], parts[1, own, :], parts[2, own, :])]
        for e in range(1, split):
            states.append(tuple(got_parts[e, i, h * rows : (h + 1) * rows, :] for i in range(3)))
        top = functools.reduce(jnp.maximum, [st[1] for st in states])
        mix = jnp.zeros((rows, HD), F32)
        tot = jnp.zeros((rows, HD), F32)
        for st in states:
            w = jnp.exp(st[1] - top)
            mix = mix + st[0] * w
            tot = tot + st[2] * w
        res = (mix / tot).astype(BF16)
        mine[:, h * HD : (h + 1) * HD] = res
        heads[me * per + h] = res

    sems = (ss, sr, fs, fr)
    out, forwards = spread(n, me, heads, None, per, sems)

    loads[2].wait()
    lhs = mine[...]

    def project(dev):
        w = wout[:, pl.ds(pl.multiple_of(dev * feats, feats), feats)]
        return jnp.dot(lhs, w, preferred_element_type=F32)

    oa = {}
    for d in order:
        out_a[d] = project(2 * chip_at(d) + 1 - core)
        oa[d] = rcopy(out_a.at[d], out_got_a.at[d], oas.at[d], oar.at[d], partner)
        oa[d].start()
    ob = {}
    for d in order:
        p = project(same(d))
        oa[d].wait_recv()
        out_b[d] = p + out_got_a[d]
        if d:
            ob[d] = rcopy(out_b.at[d], out_got_b.at[d], obs.at[d], obr.at[d], same(d))
            ob[d].start()
    pass_on(n, me, heads, per, sems, out, forwards)
    heads_out[...] = heads[...]
    total = out_b[0]
    for d in range(1, chips):
        ob[d].wait_recv()
        total = total + out_got_b[d]
    base_out[...] = total
    for c in list(a.values()) + list(b.values()) + ex + px + list(oa.values()) + list(ob.values()):
        c.wait_send()


def dma(k):
    return pltpu.SemaphoreType.DMA((k,))


def local(
    hidden_in, norm_gain, w_query, w_keyval, w_out, q_delta, q_rows, q_cols, q_count,
    o_delta, o_rows, o_cols, o_count, key_cache, value_cache, lengths,
):
    n = lax.axis_size("fsdp")
    chips = n // 2
    steps, seqs, feats = hidden_in.shape
    rows = steps * seqs
    depth, width = w_query.shape
    kv_width = w_keyval.shape[1]
    kvh = kv_width // 2 // HD
    split = n // kvh
    per = width // HD
    group = per * split
    slots = q_delta.shape[0]
    span = key_cache.shape[1]
    msg_width = width + HD
    unroll = next(u for u in (8, 6, 4, 3, 2, 1) if slots % u == 0)

    row_blocks, col_blocks = feats // BLOCK, width // BLOCK
    cap = min(4, row_blocks * col_blocks)
    packed = (n * cap, BLOCK, BLOCK)
    pack, place, over = pl.pallas_call(
        functools.partial(pack_kernel, cap, row_blocks, col_blocks),
        out_shape=(
            jax.ShapeDtypeStruct(packed, BF16),
            jax.ShapeDtypeStruct((n, 8, 128), F32),
            jax.ShapeDtypeStruct((slots,), jnp.int32),
        ),
        in_specs=[SM, SM, SM, VM],
        out_specs=(VM, VM, SM),
        scratch_shapes=[pltpu.SMEM((n,), jnp.int32)],
        compiler_params=pltpu.CompilerParams(vmem_limit_bytes=16 << 20),
        name="pack_query_delta",
    )(q_rows, q_cols, q_count, q_delta)

    normed, query, keyval, blocks, places = pl.pallas_call(
        functools.partial(gather_kernel, n, cap),
        out_shape=(
            jax.ShapeDtypeStruct((n * row_blocks, rows, BLOCK), BF16),
            jax.ShapeDtypeStruct((rows, width), F32),
            jax.ShapeDtypeStruct((rows, kv_width), F32),
            jax.ShapeDtypeStruct(packed, BF16),
            jax.ShapeDtypeStruct((n, 8, 128), F32),
        ),
        in_specs=[VM, VM, ANY, ANY, VM, VM],
        out_specs=(VM, VM, VM, VM, VM),
        scratch_shapes=[
            pltpu.VMEM((n, rows + 16, feats), BF16),
            pltpu.VMEM(w_query.shape, BF16),
            pltpu.VMEM(w_keyval.shape, BF16),
            pltpu.VMEM(packed, BF16),
            pltpu.VMEM((n, 8, 128), F32),
            dma(chips), dma(chips), dma(chips), dma(chips), dma(2),
            dma(n), dma(n), dma(n), dma(n),
        ],
        compiler_params=pltpu.CompilerParams(
            collective_id=0, has_side_effects=True, vmem_limit_bytes=24 << 20
        ),
        name="gather_norm_project",
    )(hidden_in.reshape(rows, feats), norm_gain.reshape(1, feats), w_query, w_keyval, pack, place)
    spots = places[:, :cap, 0].reshape(-1).astype(jnp.int32)

    msg, query = pl.pallas_call(
        functools.partial(query_delta_kernel, n, split, unroll, cap),
        out_shape=(
            jax.ShapeDtypeStruct((n, rows, msg_width), F32),
            jax.ShapeDtypeStruct((rows, width), F32),
        ),
        in_specs=[SM, SM, SM, SM, VM, VM, VM, VM, VM, VM],
        out_specs=(VM, VM),
        compiler_params=pltpu.CompilerParams(vmem_limit_bytes=24 << 20),
        name="query_delta",
    )(q_rows, q_cols, over, spots, normed, keyval, q_delta, query, w_query, blocks)

    position = (lengths[None, :] + jnp.arange(steps, dtype=jnp.int32)[:, None]).astype(F32)
    half = HD // 2
    freq = theta_base ** (-(jnp.arange(half, dtype=F32) * 2.0) / HD)
    angle = position.reshape(rows, 1) * freq
    cosine, sine = jnp.cos(angle), jnp.sin(angle)
    cosine = jnp.concatenate([cosine, cosine], axis=-1)
    sine = jnp.concatenate([-sine, sine], axis=-1)

    vm = pltpu.VMEM
    heads, base = pl.pallas_call(
        functools.partial(main_kernel, n, split, steps),
        out_shape=(
            jax.ShapeDtypeStruct((n * per, rows, HD), BF16),
            jax.ShapeDtypeStruct((rows, feats), F32),
        ),
        in_specs=[VM, VM, VM, VM, SM, ANY, ANY, ANY],
        out_specs=(VM, VM),
        scratch_shapes=[
            vm(key_cache.shape, BF16),
            vm(value_cache.shape, BF16),
            vm(w_out.shape, BF16),
            vm((chips, rows, msg_width), F32),
            vm((chips, rows, msg_width), F32),
            vm((chips, rows, msg_width), F32),
            vm((split, rows, msg_width), BF16),
            vm((group * rows, HD), F32),
            vm((3, group * rows, HD), F32),
            vm((split, 3, per * rows, HD), F32),
            vm((rows, width), BF16),
            vm((chips, rows, feats), F32),
            vm((chips, rows, feats), F32),
            vm((chips, rows, feats), F32),
            vm((chips, rows, feats), F32),
            vm((n * per, rows, HD), BF16),
            dma(3),
            dma(chips), dma(chips), dma(chips), dma(chips),
            dma(split), dma(split), dma(split), dma(split),
            dma(chips), dma(chips), dma(chips), dma(chips),
            dma(chips), dma(chips), dma(chips), dma(chips),
        ],
        compiler_params=pltpu.CompilerParams(
            collective_id=1, has_side_effects=True, vmem_limit_bytes=40 << 20
        ),
        name="attend_project",
    )(msg, query, cosine, sine, lengths, key_cache, value_cache, w_out)

    out = pl.pallas_call(
        functools.partial(out_delta_kernel, unroll),
        out_shape=jax.ShapeDtypeStruct((rows, feats), BF16),
        in_specs=[SM, SM, SM, VM, VM, VM],
        out_specs=VM,
        scratch_shapes=[vm((rows, feats), F32)],
        compiler_params=pltpu.CompilerParams(vmem_limit_bytes=24 << 20),
        name="out_delta",
    )(o_rows, o_cols, o_count, heads, base, o_delta)
    return out.reshape(steps, seqs, feats)


def solution(mesh):
    both = ("groups", "fsdp")
    in_specs = (
        P(None, "groups", "fsdp"),
        P("fsdp"),
        P(None, "fsdp"),
        P("fsdp", None),
        P("fsdp", None),
        P(both, None, None),
        P(both),
        P(both),
        P(both),
        P(both, None, None),
        P(both),
        P(both),
        P(both),
        P("groups", "fsdp", None),
        P("groups", "fsdp", None),
        P("groups"),
    )
    out_specs = P(None, "groups", "fsdp")
    return jax.shard_map(local, mesh=mesh, in_specs=in_specs, out_specs=out_specs, check_vma=False)
```

time: 716 us -> 142 us (0.20)
  blocking collectives: 388 us -> 0 us
  waiting for transfers between devices: 145 us -> 0 us
  Pallas kernels: 0 us -> 115 us
  local copies, waits for them, and re-layouts: 89.9 us -> 24.5 us
  matrix products: 35.9 us -> 0 us
  other arithmetic: 26.8 us -> 0.58 us
  between operations: 15.1 us -> 1.45 us
  starting transfers between devices: 8.88 us -> 0 us
    all_gather x2 -> x0, blocking collectives: 388 us -> none  [the longest x1 371 us: local(): lax.all_gather(norm_gain, 'fsdp', axis=0, tiled=True)]
    pallas_call x0 -> x5, Pallas kernels: none -> 115 us  [the longest x1 61.6 us: local(): pl.pallas_call(functools.partial(gather_kernel, n, cap), out_shape=(jax.S...]
    psum x1 -> x0, waiting for transfers between devices: 89.2 us -> none  [local(): lax.psum(jnp.dot(local_rows, w_keyval, preferred_element_type=jnp.float32...]
    reduce_scatter x1 -> x0, waiting for transfers between devices: 54.4 us -> none  [local(): lax.psum_scatter(partial_out, 'fsdp', scatter_dimension=2, tiled=True)]
    convert_element_type x4 -> x2, local copies, waits for them, and re-layouts: 48.7 us -> 0.17 us  [the longest x1 0.09 us: local(): spots = places[:, :cap, 0].reshape(-1).astype(jnp.int32)]
    dot_general x9 -> x0, matrix products: 35.9 us -> none  [the longest x2 12.5 us: spread_blocks(): jnp.dot(table, flat, preferred_element_type=jnp.float32)]
    concatenate x2 -> x1, other arithmetic: 13.8 us -> 0.08 us  [local(): cosine = jnp.concatenate([cosine, cosine], axis=-1)]
    dot_general x2 -> x0, local copies, waits for them, and re-layouts: 12 us -> none  [the longest x1 12 us: local(): jnp.dot(flat, merged_q, preferred_element_type=jnp.float32)]
  transfers between devices with their start and end apart: 7 -> 0, of which waited for: 3 -> 0; matrix products, arithmetic and copies ran while one was open for 7% -> 0% of each run, Pallas kernels for 0% -> 0%
where the time goes in v1:
time: 142 us; the launch traced here: 141 us
  Pallas kernels  115 us (81%)
  local copies, waits for them, and re-layouts  24.5 us (17%)
  between operations  1.45 us (1%)
    pallas_call x1, Pallas kernels, local(): pl.pallas_call(functools.partial(gather_kernel, n, cap), out_shape=(jax.S...  61.6 us
    pallas_call x1, Pallas kernels, local(): pl.pallas_call(functools.partial(main_kernel, n, split, steps), out_shape...  44.4 us
    unnamed x46, local copies, waits for them, and re-layouts  23.6 us
    pallas_call x1, Pallas kernels, local(): pl.pallas_call(functools.partial(query_delta_kernel, n, split, unroll, ca...  3.87 us

profile of v1, /device:TPU:29, one launch (start us, length us, event | category | flops | bytes accessed | tf_op | source)
XLA Modules:
  0.0 141.1 jit_solution(4696407991125036768)
XLA Ops:
  0.7 0.0 copy-start.3
  0.7 1.4 copy-done.3
  2.1 0.0 copy-start.14
  2.1 0.7 copy-done.14
  2.7 0.0 copy-start.16
  2.7 0.7 copy-done.16
  3.4 2.4 %pack_query_delta.1 = (bf16[64,128,128]{2,1,0:T(8,128)(2,1)S(1)}, f32[16,8,128]{2,1,0:T(8,128)S(1)}, s32[48]{0:T(128)S(1)}) custom-call(s32[48]{0:T(128)S(1)} %copy-done.14, s32[48]{0:T(128)S(1)} %copy-done.16, s32[1]{0:T(128)S(6)} %copy.17.count_ref, bf16[48,128,128]{2,1,0:T(8,128)(2,1)S(1)} %copy-done.3), custom_call_target="tpu_custom_call" | custom-call | tf_op jit(solution)/shard_map/pack_query_delta/pallas_call | solution.py:444
  5.8 0.0 copy-start.21
  5.8 0.7 reshape.36.gain_ref
  6.5 0.0 copy-done.21
  6.5 0.0 copy-start
  6.5 3.4 %copy-done = bf16[8192,512]{1,0:T(8,128)(2,1)S(1)} copy-done((bf16[8192,512]{1,0:T(8,128)(2,1)S(1)}, bf16[8192,512]{1,0:T(8,128)(2,1)}, u32[]{:S(2)}) %copy-start) | copy-done | bytes 8388632
  9.9 0.0 copy-start.5
  9.9 1.6 %copy-done.5 = bf16[512,2048]{1,0:T(8,128)(2,1)S(1)} copy-done((bf16[512,2048]{1,0:T(8,128)(2,1)S(1)}, bf16[512,2048]{1,0:T(8,128)(2,1)}, u32[]{:S(2)}) %copy-start.5) | copy-done | bytes 2097176
  11.5 0.0 copy-start.13
  11.5 0.8 copy-done.13
  12.2 0.0 copy-start.4
  12.2 0.0 copy-start.15
  12.2 0.0 copy-start.17
  12.2 61.6 %gather_norm_project.1 = (bf16[64,32,128]{2,1,0:T(8,128)(2,1)S(1)}, f32[32,512]{1,0:T(8,128)S(1)}, f32[32,2048]{1,0:T(8,128)S(1)}, bf16[64,128,128]{2,1,0:T(8,128)(2,1)S(1)}, f32[16,8,128]{2,1,0:T(8,128)S(1)}) custom-call(bf16[32,512]{1,0:T(8,128)(2,1)S(1)} %bitcast.2, bf16[1,512]{1,0:T(2,128)(2,1)S(1)} %reshape.36.gain_ref, bf16[8192,512]{1,0:T(8,128)(2,1)S(1)} %copy-done, ...), custom_call_target="tpu_custom_call" | custom-call | tf_op jit(solution)/shard_map/gather_norm_project/pallas_call | solution.py:458
  73.9 0.0 copy-start.8
  73.9 1.3 copy-done.8
  75.2 0.0 copy-start.11
  75.2 0.7 copy-done.11
  75.9 0.3 convert_reduce_fusion
  76.2 0.1 convert_element_type.16.spot_ref
  76.3 0.0 copy-done.4
  76.4 0.0 copy-done.15
  76.4 0.0 copy-done.17
  76.4 0.0 copy-start.1
  76.4 3.4 %copy-done.1 = bf16[8192,512]{1,0:T(8,128)(2,1)S(1)} copy-done((bf16[8192,512]{1,0:T(8,128)(2,1)S(1)}, bf16[8192,512]{1,0:T(8,128)(2,1)}, u32[]{:S(2)}) %copy-start.1) | copy-done | bytes 8388632
  79.8 0.0 copy-start.9
  79.8 1.6 %copy-done.9 = bf16[64,128,128]{2,1,0:T(8,128)(2,1)S(1)} copy-done((bf16[64,128,128]{2,1,0:T(8,128)(2,1)S(1)}, bf16[64,128,128]{2,1,0:T(8,128)(2,1)}, u32[]{:S(2)}) %copy-start.9) | copy-done | bytes 2097176
  81.3 0.0 copy-start.12
  81.4 0.9 copy-done.12
  82.3 0.0 copy-start.22
  82.3 0.7 copy-done.22
  83.0 0.0 copy-start.18
  83.0 3.9 %query_delta.1 = (f32[16,32,640]{2,1,0:T(8,128)S(1)}, f32[32,512]{1,0:T(8,128)S(1)}) custom-call(s32[48]{0:T(128)S(1)} %copy-done.15, s32[48]{0:T(128)S(1)} %copy-done.17, s32[48]{0:T(128)S(1)} %copy-done.22, s32[64]{0:T(128)S(1)} %convert_element_type.16.spot_ref, bf16[64,32,128]{2,1,0:T(8,128)(2,1)S(1)} %get-tuple-element.21.all_ref, ...), custom_call_target="tpu_custom_call" | custom-call | tf_op jit(solution)/shard_map/query_delta/pallas_call | solution.py:485
  86.8 0.0 copy-done.18
  86.8 0.1 convert_element_type.18
  86.9 0.1 fusion
  87.1 0.1 pad_maximum_fusion
  87.2 0.0 copy-start.2
  87.2 3.4 %copy-done.2 = bf16[512,8192]{1,0:T(8,128)(2,1)S(1)} copy-done((bf16[512,8192]{1,0:T(8,128)(2,1)S(1)}, bf16[512,8192]{1,0:T(8,128)(2,1)}, u32[]{:S(2)}) %copy-start.2) | copy-done | bytes 8388632
  90.6 0.0 copy-start.6
  90.6 1.6 %copy-done.6 = bf16[16,512,128]{2,1,0:T(8,128)(2,1)S(1)} copy-done((bf16[16,512,128]{2,1,0:T(8,128)(2,1)S(1)}, bf16[16,512,128]{2,1,0:T(8,128)(2,1)}, u32[]{:S(2)}) %copy-start.6) | copy-done | bytes 2097176
  92.2 0.0 copy-start.7
  92.2 1.6 %copy-done.7 = bf16[16,512,128]{2,1,0:T(8,128)(2,1)S(1)} copy-done((bf16[16,512,128]{2,1,0:T(8,128)(2,1)S(1)}, bf16[16,512,128]{2,1,0:T(8,128)(2,1)}, u32[]{:S(2)}) %copy-start.7) | copy-done | bytes 2097176
  93.7 0.0 copy-start.10
  93.7 0.0 copy-start.19
  93.8 0.0 copy-start.20
  93.8 44.4 %attend_project.1 = (bf16[64,32,128]{2,1,0:T(8,128)(2,1)S(1)}, f32[32,512]{1,0:T(8,128)S(1)}) custom-call(f32[16,32,640]{2,1,0:T(8,128)S(1)} %get-tuple-element.25.msg, f32[32,512]{1,0:T(8,128)S(1)} %get-tuple-element.26.q_ref, f32[32,128]{1,0:T(8,128)S(1)} %get-tuple-element.32.cos_ref, f32[32,128]{1,0:T(8,128)S(1)} %get-tuple-element.33.sin_ref, ...), custom_call_target="tpu_custom_call" | custom-call | tf_op jit(solution)/shard_map/attend_project/pallas_call | solution.py:506
  138.8 0.0 copy-done.10
  138.8 0.0 copy-done.19
  138.8 0.0 copy-done.20
  138.8 2.3 %out_delta.1 = bf16[32,512]{1,0:T(8,128)(2,1)} custom-call(s32[48]{0:T(128)S(1)} %copy-done.19, s32[48]{0:T(128)S(1)} %copy-done.20, s32[1]{0:T(128)S(6)} %copy.18.count_ref, bf16[64,32,128]{2,1,0:T(8,128)(2,1)S(1)} %get-tuple-element.27.heads_ref, f32[32,512]{1,0:T(8,128)S(1)} %get-tuple-element.28.base_ref, bf16[48,128,128]{2,1,0:T(8,128)(2,1)S(1)} %copy-done.10), custom_call_target="tpu_custom_call" | custom-call | tf_op jit(solution)/shard_map/out_delta/pallas_call | solution.py:543
  (2 shorter events, 0.0 us)
Async XLA Ops:
  0.7 1.4 copy-start.3
  2.1 0.7 copy-start.14
  2.7 0.7 copy-start.16
  5.8 0.7 copy-start.21
  6.5 3.4 %copy-start = (bf16[8192,512]{1,0:T(8,128)(2,1)S(1)}, bf16[8192,512]{1,0:T(8,128)(2,1)}, u32[]{:S(2)}) copy-start(bf16[8192,512]{1,0:T(8,128)(2,1)} %w_ref.1) | copy-start | bytes 25165828
  9.9 1.6 %copy-start.5 = (bf16[512,2048]{1,0:T(8,128)(2,1)S(1)}, bf16[512,2048]{1,0:T(8,128)(2,1)}, u32[]{:S(2)}) copy-start(bf16[512,2048]{1,0:T(8,128)(2,1)} %wkv_hbm.1) | copy-start | bytes 6291460
  11.5 0.8 copy-start.13
  12.2 64.1 %copy-start.4 = (bf16[48,128,128]{2,1,0:T(8,128)(2,1)S(1)}, bf16[48,128,128]{2,1,0:T(8,128)(2,1)}, u32[]{:S(2)}) copy-start(bf16[48,128,128]{2,1,0:T(8,128)(2,1)} %delta_ref.4) | copy-start | bytes 4718596
  12.2 64.1 %copy-start.15 = (s32[48]{0:T(128)S(1)}, s32[48]{0:T(128)}, u32[]{:S(2)}) copy-start(s32[48]{0:T(128)} %rows_ref.4) | copy-start | bytes 580
  12.2 64.1 %copy-start.17 = (s32[48]{0:T(128)S(1)}, s32[48]{0:T(128)}, u32[]{:S(2)}) copy-start(s32[48]{0:T(128)} %cols_ref.4) | copy-start | bytes 580
  73.9 1.3 copy-start.8
  75.2 0.7 copy-start.11
  76.4 3.4 %copy-start.1 = (bf16[8192,512]{1,0:T(8,128)(2,1)S(1)}, bf16[8192,512]{1,0:T(8,128)(2,1)}, u32[]{:S(2)}) copy-start(bf16[8192,512]{1,0:T(8,128)(2,1)} %w_ref.1) | copy-start | bytes 25165828
  79.8 1.6 %copy-start.9 = (bf16[64,128,128]{2,1,0:T(8,128)(2,1)S(1)}, bf16[64,128,128]{2,1,0:T(8,128)(2,1)}, u32[]{:S(2)}) copy-start(bf16[64,128,128]{2,1,0:T(8,128)(2,1)} %copy-done.8) | copy-start | bytes 6291460
  81.3 0.9 copy-start.12
  82.3 0.7 copy-start.22
  83.0 3.9 %copy-start.18 = (s32[16]{0:T(128)S(1)}, s32[16]{0:T(128)}, u32[]{:S(2)}) copy-start(s32[16]{0:T(128)} %len_ref.1) | copy-start | bytes 196
  87.2 3.4 %copy-start.2 = (bf16[512,8192]{1,0:T(8,128)(2,1)S(1)}, bf16[512,8192]{1,0:T(8,128)(2,1)}, u32[]{:S(2)}) copy-start(bf16[512,8192]{1,0:T(8,128)(2,1)} %wout_hbm.1) | copy-start | bytes 25165828
  90.6 1.6 %copy-start.6 = (bf16[16,512,128]{2,1,0:T(8,128)(2,1)S(1)}, bf16[16,512,128]{2,1,0:T(8,128)(2,1)}, u32[]{:S(2)}) copy-start(bf16[16,512,128]{2,1,0:T(8,128)(2,1)} %keys_hbm.1) | copy-start | bytes 6291460
  92.2 1.6 %copy-start.7 = (bf16[16,512,128]{2,1,0:T(8,128)(2,1)S(1)}, bf16[16,512,128]{2,1,0:T(8,128)(2,1)}, u32[]{:S(2)}) copy-start(bf16[16,512,128]{2,1,0:T(8,128)(2,1)} %values_hbm.1) | copy-start | bytes 6291460
  93.7 45.0 %copy-start.10 = (bf16[48,128,128]{2,1,0:T(8,128)(2,1)S(1)}, bf16[48,128,128]{2,1,0:T(8,128)(2,1)}, u32[]{:S(2)}) copy-start(bf16[48,128,128]{2,1,0:T(8,128)(2,1)} %delta_ref.5) | copy-start | bytes 4718596
  93.7 45.1 %copy-start.19 = (s32[48]{0:T(128)S(1)}, s32[48]{0:T(128)}, u32[]{:S(2)}) copy-start(s32[48]{0:T(128)} %rows_ref.5) | copy-start | bytes 580
  93.8 45.1 %copy-start.20 = (s32[48]{0:T(128)S(1)}, s32[48]{0:T(128)}, u32[]{:S(2)}) copy-start(s32[48]{0:T(128)} %cols_ref.5) | copy-start | bytes 580

commit v2 on v1

--- a/solution.py
+++ b/solution.py
@@ -172,9 +172,11 @@
 
 def query_delta_kernel(
     n, split, unroll, cap, rows_ref, cols_ref, over_ref, spot_ref, all_ref, kv_ref, delta_ref,
-    q_ref, w_ref, got_ref, msg_ref, query_ref
+    q_ref, w_hbm, got_ref, msg_ref, query_ref, w_ref, load_sem
 ):
     me = lax.axis_index("fsdp")
+    load = pltpu.make_async_copy(w_hbm, w_ref, load_sem.at[0])
+    load.start()
     blocks = all_ref.shape[0] // n
     slots = delta_ref.shape[0]
     width = msg_ref.shape[2] - HD
@@ -184,7 +186,23 @@
         at = (j % 2) * half + (j // split) * HD
         msg_ref[j, :, 0:width] = jnp.zeros((msg_ref.shape[1], width), F32)
         msg_ref[j, :, width : width + HD] = kv_ref[:, at : at + HD]
+    @pl.loop(0, slots // unroll)
+    def _(step):
+        done = []
+        for u in range(unroll):
+            k = step * unroll + u
+            r = jnp.clip(rows_ref[k] - me * blocks, 0, blocks - 1)
+            lhs = all_ref[me * blocks + r]
+            lhs = jnp.where(over_ref[k] > 0, lhs, jnp.zeros_like(lhs))
+            done.append(jnp.dot(lhs, delta_ref[k], preferred_element_type=F32))
+        for u in range(unroll):
+            c = cols_ref[step * unroll + u]
+            at = pl.ds(pl.multiple_of(lax.rem(c, per) * BLOCK, BLOCK), BLOCK)
+            j = lax.div(c, per)
+            msg_ref[j, :, at] = msg_ref[j, :, at] + done[u]
+
     query_ref[...] = q_ref[...]
+    load.wait()
     group = next(u for u in (8, 4, 2, 1) if (n * cap) % u == 0)
 
     @pl.loop(0, n * cap // group)
@@ -207,21 +225,6 @@
             )
         for at, term in done:
             query_ref[:, at] = query_ref[:, at] + term
-
-    @pl.loop(0, slots // unroll)
-    def _(step):
-        done = []
-        for u in range(unroll):
-            k = step * unroll + u
-            r = jnp.clip(rows_ref[k] - me * blocks, 0, blocks - 1)
-            lhs = all_ref[me * blocks + r]
-            lhs = jnp.where(over_ref[k] > 0, lhs, jnp.zeros_like(lhs))
-            done.append(jnp.dot(lhs, delta_ref[k], preferred_element_type=F32))
-        for u in range(unroll):
-            c = cols_ref[step * unroll + u]
-            at = pl.ds(pl.multiple_of(lax.rem(c, per) * BLOCK, BLOCK), BLOCK)
-            j = lax.div(c, per)
-            msg_ref[j, :, at] = msg_ref[j, :, at] + done[u]
 
 
 def out_delta_kernel(unroll, rows_ref, cols_ref, count_ref, heads_ref, base_ref, delta_ref, out_ref, acc):
@@ -476,7 +479,7 @@
             dma(n), dma(n), dma(n), dma(n),
         ],
         compiler_params=pltpu.CompilerParams(
-            collective_id=0, has_side_effects=True, vmem_limit_bytes=24 << 20
+            collective_id=0, has_side_effects=True, vmem_limit_bytes=54 << 20
         ),
         name="gather_norm_project",
     )(hidden_in.reshape(rows, feats), norm_gain.reshape(1, feats), w_query, w_keyval, pack, place)
@@ -488,9 +491,10 @@
             jax.ShapeDtypeStruct((n, rows, msg_width), F32),
             jax.ShapeDtypeStruct((rows, width), F32),
         ),
-        in_specs=[SM, SM, SM, SM, VM, VM, VM, VM, VM, VM],
+        in_specs=[SM, SM, SM, SM, VM, VM, VM, VM, ANY, VM],
         out_specs=(VM, VM),
-        compiler_params=pltpu.CompilerParams(vmem_limit_bytes=24 << 20),
+        scratch_shapes=[pltpu.VMEM(w_query.shape, BF16), dma(1)],
+        compiler_params=pltpu.CompilerParams(vmem_limit_bytes=52 << 20),
         name="query_delta",
     )(q_rows, q_cols, over, spots, normed, keyval, q_delta, query, w_query, blocks)
 
@@ -535,7 +539,7 @@
             dma(chips), dma(chips), dma(chips), dma(chips),
         ],
         compiler_params=pltpu.CompilerParams(
-            collective_id=1, has_side_effects=True, vmem_limit_bytes=40 << 20
+            collective_id=1, has_side_effects=True, vmem_limit_bytes=57 << 20
         ),
         name="attend_project",
     )(msg, query, cosine, sine, lengths, key_cache, value_cache, w_out)

time: 142 us -> 138 us (0.972)
  local copies, waits for them, and re-layouts: 24.5 us -> 11.4 us
  Pallas kernels: 115 us -> 122 us
  other arithmetic: 0.58 us -> 2.05 us
    unnamed x46 -> x34, local copies, waits for them, and re-layouts: 23.6 us -> 9.98 us
    pallas_call x1, Pallas kernels: 3.87 us -> 8.55 us  [local(): pl.pallas_call(functools.partial(query_delta_kernel, n, split, unroll, ca...]
    pallas_call x1, Pallas kernels: 61.6 us -> 63.7 us  [local(): pl.pallas_call(functools.partial(gather_kernel, n, cap), out_shape=(jax.S...]
where the time goes in v2:
time: 138 us; the launch traced here: 137 us
  Pallas kernels  122 us (88%)
  local copies, waits for them, and re-layouts  11.4 us (8%)
  other arithmetic  2.05 us (1%)
  between operations  1.44 us (1%)
    pallas_call x1, Pallas kernels, local(): pl.pallas_call(functools.partial(gather_kernel, n, cap), out_shape=(jax.S...  63.7 us
    pallas_call x1, Pallas kernels, local(): pl.pallas_call(functools.partial(main_kernel, n, split, steps), out_shape...  45.3 us
    unnamed x34, local copies, waits for them, and re-layouts  9.98 us
    pallas_call x1, Pallas kernels, local(): pl.pallas_call(functools.partial(query_delta_kernel, n, split, unroll, ca...  8.55 us

profile of v2, /device:TPU:29, one launch (start us, length us, event | category | flops | bytes accessed | tf_op | source)
XLA Modules:
  0.0 137.3 jit_solution(3904847787096074310)
XLA Ops:
  0.7 0.0 copy-start
  0.7 1.4 %copy-done = bf16[48,128,128]{2,1,0:T(8,128)(2,1)S(1)} copy-done((bf16[48,128,128]{2,1,0:T(8,128)(2,1)S(1)}, bf16[48,128,128]{2,1,0:T(8,128)(2,1)}, u32[]{:S(2)}) %copy-start) | copy-done | bytes 1572888
  2.1 0.0 copy-start.10
  2.1 0.7 copy-done.10
  2.7 0.0 copy-start.12
  2.7 0.7 copy-done.12
  3.4 2.5 %pack_query_delta.1 = (bf16[64,128,128]{2,1,0:T(8,128)(2,1)S(1)}, f32[16,8,128]{2,1,0:T(8,128)S(1)}, s32[48]{0:T(128)S(1)}) custom-call(s32[48]{0:T(128)S(1)} %copy-done.10, s32[48]{0:T(128)S(1)} %copy-done.12, s32[1]{0:T(128)S(6)} %copy.17.count_ref, bf16[48,128,128]{2,1,0:T(8,128)(2,1)S(1)} %copy-done), custom_call_target="tpu_custom_call" | custom-call | tf_op jit(solution)/shard_map/pack_query_delta/pallas_call | solution.py:447
  5.9 0.0 copy-start.1
  5.9 1.3 copy-done.1
  7.2 0.0 copy-start.8
  7.2 0.6 copy-done.8
  7.9 1.3 reshape.36.gain_ref
  9.1 0.0 copy-start.11
  9.1 0.0 copy-start.13
  9.1 63.7 %gather_norm_project.1 = (bf16[64,32,128]{2,1,0:T(8,128)(2,1)}, f32[32,512]{1,0:T(8,128)}, f32[32,2048]{1,0:T(8,128)}, bf16[64,128,128]{2,1,0:T(8,128)(2,1)}, f32[16,8,128]{2,1,0:T(8,128)}) custom-call(bf16[32,512]{1,0:T(8,128)(2,1)} %bitcast.2, bf16[1,512]{1,0:T(2,128)(2,1)} %reshape.36.gain_ref, bf16[8192,512]{1,0:T(8,128)(2,1)} %w_hbm.1, ...), custom_call_target="tpu_custom_call" | custom-call | tf_op jit(solution)/shard_map/gather_norm_project/pallas_call | solution.py:461
  72.9 1.2 convert_reduce_fusion
  74.0 0.1 convert_element_type.16.spot_ref
  74.1 0.0 copy-done.11
  74.2 0.0 copy-done.13
  74.2 0.0 copy-start.4
  74.2 1.0 copy-done.4
  75.2 0.0 copy-start.5
  75.2 0.9 copy-done.5
  76.2 0.0 copy-start.7
  76.2 0.8 copy-done.7
  77.0 0.0 copy-start.16
  77.0 8.5 %query_delta.1 = (f32[16,32,640]{2,1,0:T(8,128)}, f32[32,512]{1,0:T(8,128)S(1)}) custom-call(s32[48]{0:T(128)S(1)} %copy-done.11, s32[48]{0:T(128)S(1)} %copy-done.13, s32[48]{0:T(128)S(1)} %get-tuple-element.17.over_ref, s32[64]{0:T(128)S(1)} %convert_element_type.16.spot_ref, bf16[64,32,128]{2,1,0:T(8,128)(2,1)S(1)} %copy-done.4, ...), custom_call_target="tpu_custom_call" | custom-call | tf_op jit(solution)/shard_map/query_delta/pallas_call | solution.py:488
  85.6 0.0 copy-start.6
  85.6 0.6 copy-done.6
  86.2 0.0 copy-done.16
  86.2 0.1 convert_element_type.18
  86.3 0.1 fusion
  86.4 0.7 pad_maximum_fusion
  87.1 0.0 copy-start.2
  87.1 0.0 copy-start.14
  87.1 0.0 copy-start.15
  87.1 45.3 %attend_project.1 = (bf16[64,32,128]{2,1,0:T(8,128)(2,1)}, f32[32,512]{1,0:T(8,128)}) custom-call(f32[16,32,640]{2,1,0:T(8,128)} %get-tuple-element.25.msg, f32[32,512]{1,0:T(8,128)} %copy-done.6, f32[32,128]{1,0:T(8,128)} %get-tuple-element.32.cos_ref, f32[32,128]{1,0:T(8,128)} %get-tuple-element.33.sin_ref, s32[16]{0:T(128)} %len_ref.1, ...), custom_call_target="tpu_custom_call" | custom-call | tf_op jit(solution)/shard_map/attend_project/pallas_call | solution.py:510
  133.1 0.0 copy-done.2
  133.1 0.0 copy-done.14
  133.1 0.0 copy-done.15
  133.1 0.0 copy-start.3
  133.2 1.0 copy-done.3
  134.2 0.0 copy-start.9
  134.2 0.8 copy-done.9
  135.0 2.3 %out_delta.1 = bf16[32,512]{1,0:T(8,128)(2,1)} custom-call(s32[48]{0:T(128)S(1)} %copy-done.14, s32[48]{0:T(128)S(1)} %copy-done.15, s32[1]{0:T(128)S(6)} %copy.18.count_ref, bf16[64,32,128]{2,1,0:T(8,128)(2,1)S(1)} %copy-done.3, f32[32,512]{1,0:T(8,128)S(1)} %copy-done.9, bf16[48,128,128]{2,1,0:T(8,128)(2,1)S(1)} %copy-done.2), custom_call_target="tpu_custom_call" | custom-call | tf_op jit(solution)/shard_map/out_delta/pallas_call | solution.py:547
  (2 shorter events, 0.0 us)
Async XLA Ops:
  0.7 1.4 %copy-start = (bf16[48,128,128]{2,1,0:T(8,128)(2,1)S(1)}, bf16[48,128,128]{2,1,0:T(8,128)(2,1)}, u32[]{:S(2)}) copy-start(bf16[48,128,128]{2,1,0:T(8,128)(2,1)} %delta_ref.4) | copy-start | bytes 4718596
  2.1 0.7 copy-start.10
  2.7 0.7 copy-start.12
  5.9 1.3 copy-start.1
  7.2 0.6 copy-start.8
  9.1 65.0 %copy-start.11 = (s32[48]{0:T(128)S(1)}, s32[48]{0:T(128)}, u32[]{:S(2)}) copy-start(s32[48]{0:T(128)} %rows_ref.4) | copy-start | bytes 580
  9.1 65.0 %copy-start.13 = (s32[48]{0:T(128)S(1)}, s32[48]{0:T(128)}, u32[]{:S(2)}) copy-start(s32[48]{0:T(128)} %cols_ref.4) | copy-start | bytes 580
  74.2 1.0 copy-start.4
  75.2 0.9 copy-start.5
  76.2 0.8 copy-start.7
  77.0 9.2 %copy-start.16 = (s32[16]{0:T(128)S(1)}, s32[16]{0:T(128)}, u32[]{:S(2)}) copy-start(s32[16]{0:T(128)} %len_ref.1) | copy-start | bytes 196
  85.6 0.6 copy-start.6
  87.1 46.0 %copy-start.2 = (bf16[48,128,128]{2,1,0:T(8,128)(2,1)S(1)}, bf16[48,128,128]{2,1,0:T(8,128)(2,1)}, u32[]{:S(2)}) copy-start(bf16[48,128,128]{2,1,0:T(8,128)(2,1)} %delta_ref.5) | copy-start | bytes 4718596
  87.1 46.0 %copy-start.14 = (s32[48]{0:T(128)S(1)}, s32[48]{0:T(128)}, u32[]{:S(2)}) copy-start(s32[48]{0:T(128)} %rows_ref.5) | copy-start | bytes 580
  87.1 46.0 %copy-start.15 = (s32[48]{0:T(128)S(1)}, s32[48]{0:T(128)}, u32[]{:S(2)}) copy-start(s32[48]{0:T(128)} %cols_ref.5) | copy-start | bytes 580
  133.1 1.0 copy-start.3
  134.2 0.8 copy-start.9
